TPU v7x, 32 devices: a whole 2x2x4 slice. The times are simulated.
32 devices in a mesh: groups: 2 (over y), branch: 4 (over z), head: 2 (over x), seq: 2 (over core).
Axes of the slice: x: 2, y: 2, z: 4, core: 2. Of those that a mesh axis runs over, the one named last changes fastest.
Arguments:
- queries: bfloat16 [32, 2, 64, 576], P(('groups', 'branch'), None, 'head'), parts along dimension 0, may hold values from -48 to 48
- kv_new: bfloat16 [32, 2, 576], P(('groups', 'branch')), parts along dimension 0, may hold values from -6 to 6
- cache: bfloat16 [1024, 128, 576], P(('groups', 'branch', 'seq')), parts along dimension 0, may hold values from -6 to 6
- block_list: int32 [32, 128], P('groups'), parts along dimension 0, may hold values from 0 to 511, as said below
- lengths: int32 [32], P('groups'), parts along dimension 0, may hold values from 128 to 16384
- parent: int32 [32], P('groups'), parts along dimension 0, may hold values from -1 to 14, as said below
- w_uv: bfloat16 [64, 512, 128], P('head'), may hold values from -6 to 6
- w_out: bfloat16 [8192, 3584], P('head', 'seq'), may hold values from -0.0625 to 0.0625
Outputs:
- branch_out: bfloat16 [32, 2, 3584], P(('groups', 'branch', 'head'), None, 'seq'), parts along dimension 0
There are 2 independent parts, one for each index of `groups`. A program takes and returns all parts, laid end to end along the dimension named above; an argument that names none is the same for every part. Nothing has to cross between parts.
Inputs may be any that keep to these rules, and one draw needn't show every extreme that they name: `block_list`: each branch lists 128 distinct blocks; block g is held by device g // 64 in the order of branch+seq. The blocks listed by the 4 branches of one branch index include at most 16 distinct blocks of any one holder, and exactly 16 of some holder. parent[0] is -1 (no parent); every other branch b has a parent below b.
All inputs are finite; a program needn't handle non-finite values.
Results may differ from a plain program's by a relative error of at most 0.015.
Values may be sent and summed in bfloat16 or wider, within the bound.
A program may use at most 192 MiB of HBM per device.

v0:
```python
import jax
import jax.numpy as jnp
from jax import lax
from jax.sharding import PartitionSpec as P

ROPE = 64
VHEAD = 128


def joined(shard, axis, join):
    gathered = jax.tree.map(
        lambda a, kind: lax.all_gather(a.astype(kind), axis),
        shard,
        (jnp.bfloat16, jnp.bfloat16, jnp.bfloat16),
    )

    def take(source):
        return jax.tree.map(
            lambda a, own: lax.dynamic_index_in_dim(a, source, 0, False).astype(own.dtype),
            gathered,
            shard,
        )

    return lax.fori_loop(
        1, lax.axis_size(axis), lambda source, state: join(state, take(source)), take(0)
    )


def slot_table(entries, holder, block_count, slot_count):
    targets = holder[:, None] * block_count + jnp.arange(block_count)[None, :]
    wanted = jnp.any(entries[:, :, None] == targets[:, None, :], axis=1)
    ranked = jnp.cumsum(wanted.astype(jnp.int32), axis=1) - 1
    return wanted[:, None, :] & (ranked[:, None, :] == jnp.arange(slot_count)[None, :, None])


def combine_halves(earlier, later):
    peak_one, total_one, summed_one = earlier
    peak_two, total_two, summed_two = later
    larger = jnp.maximum(peak_one, peak_two)
    scale_one = jnp.exp(peak_one - larger)
    scale_two = jnp.exp(peak_two - larger)
    return (
        larger,
        total_one * scale_one + total_two * scale_two,
        summed_one * scale_one[..., None] + summed_two * scale_two[..., None],
    )


def local(queries, kv_new, cache, block_list, lengths, parent, w_uv, w_out):
    branch_rows = queries.shape[0]
    head_local = queries.shape[2]
    feature = queries.shape[3]
    block_count = cache.shape[0]
    block_len = cache.shape[1]
    list_len = block_list.shape[1]
    latent = w_uv.shape[1]
    branch_count = lax.axis_size("branch")
    seq_count = lax.axis_size("seq")
    head_count = lax.axis_size("head")
    dev_count = branch_count * seq_count
    per_half = list_len // seq_count
    slot_count = (list_len + dev_count - 1) // dev_count
    branch_at = lax.axis_index("branch")
    seq_at = lax.axis_index("seq")
    my_index = branch_at * seq_count + seq_at
    qk_scale = float(VHEAD + ROPE) ** (-0.5)
    flat_cache = cache.reshape(block_count, block_len * feature)
    grouped = block_list.reshape(branch_count, branch_rows, seq_count, per_half).transpose(
        0, 2, 1, 3
    )
    grouped = grouped.reshape(dev_count, branch_rows * per_half)
    outgoing = slot_table(
        grouped, jnp.full((dev_count,), my_index, jnp.int32), block_count, slot_count
    )
    buffer = jnp.einsum(
        "qtk,kx->qtx",
        outgoing.astype(jnp.bfloat16),
        flat_cache,
        preferred_element_type=jnp.bfloat16,
    )
    buffer = buffer.reshape(dev_count, slot_count, block_len, feature)
    arrived = lax.all_to_all(buffer, ("branch", "seq"), split_axis=0, concat_axis=0, tiled=True)
    my_ids = lax.dynamic_slice(
        block_list, (branch_at * branch_rows, seq_at * per_half), (branch_rows, per_half)
    )
    holders = jnp.arange(dev_count, dtype=jnp.int32)
    positions = seq_at * per_half + jnp.arange(per_half)
    key_rows = arrived.reshape(-1, feature)
    peer_count = holders.shape[0]
    incoming = slot_table(
        jnp.broadcast_to(my_ids.reshape(1, -1), (peer_count, my_ids.size)),
        holders,
        block_count,
        slot_count,
    )
    targets = holders[:, None] * block_count + jnp.arange(block_count)[None, :]
    slot_ids = (jnp.sum(jnp.where(incoming, targets[:, None, :] + 1, 0), axis=-1) - 1).reshape(-1)
    matches = (my_ids[:, :, None] == slot_ids[None, None, :]) & (slot_ids >= 0)[None, None, :]
    entry_at = jnp.sum(jnp.where(matches, positions[None, :, None] + 1, 0), axis=1) - 1
    my_lengths = lax.dynamic_slice_in_dim(lengths, branch_at * branch_rows, branch_rows)
    offsets = entry_at[:, :, None] * block_len + jnp.arange(block_len)[None, None, :]
    visible = ((entry_at[:, :, None] >= 0) & (offsets < my_lengths[:, None, None])).reshape(
        branch_rows, -1
    )
    everyone = lax.all_gather(kv_new, "branch", axis=0, tiled=True)
    my_parents = lax.dynamic_slice_in_dim(parent, branch_at * branch_rows, branch_rows)
    parent_keys = jnp.take(everyone, jnp.maximum(my_parents, 0), axis=0)
    new_keys = jnp.concatenate([parent_keys, kv_new], axis=1)
    is_first = seq_at == 0
    draft_pos = jnp.arange(2)
    own_mask = jnp.broadcast_to(
        (draft_pos[None, :] <= draft_pos[:, None])[None], (branch_rows, 2, 2)
    )
    parent_mask = jnp.broadcast_to((my_parents >= 0)[:, None, None], (branch_rows, 2, 2))
    new_mask = jnp.concatenate([parent_mask, own_mask], axis=2) & is_first
    scores = (
        jnp.einsum("rtha,ka->rthk", queries, key_rows, preferred_element_type=jnp.float32)
        * qk_scale
    )
    scores = jnp.where(visible[:, None, None, :], scores, -1e30)
    new_scores = (
        jnp.einsum("rtha,rua->rthu", queries, new_keys, preferred_element_type=jnp.float32)
        * qk_scale
    )
    new_scores = jnp.where(new_mask[:, :, None, :], new_scores, -1e30)
    peak = jnp.maximum(jnp.max(scores, axis=-1), jnp.max(new_scores, axis=-1))
    exps = jnp.where(visible[:, None, None, :], jnp.exp(scores - peak[..., None]), 0.0)
    new_exps = jnp.where(new_mask[:, :, None, :], jnp.exp(new_scores - peak[..., None]), 0.0)
    totals = jnp.sum(exps, axis=-1) + jnp.sum(new_exps, axis=-1)
    summed = jnp.einsum(
        "rthk,kc->rthc",
        exps.astype(jnp.bfloat16),
        key_rows[:, :latent],
        preferred_element_type=jnp.float32,
    )
    summed = summed + jnp.einsum(
        "rthu,ruc->rthc",
        new_exps.astype(jnp.bfloat16),
        new_keys[:, :, :latent],
        preferred_element_type=jnp.float32,
    )
    wide_uv = w_uv.astype(jnp.float32)
    peak_all, totals_all, summed_all = joined((peak, totals, summed), "seq", combine_halves)
    latent_out = summed_all / totals_all[..., None]
    head_out = jnp.einsum(
        "rthc,hcv->rthv", latent_out, wide_uv, precision=lax.Precision.HIGHEST
    ).astype(jnp.bfloat16)
    flattened = head_out.reshape(
        lax.axis_size("head") * (branch_rows // head_count) * 2, head_local * head_out.shape[-1]
    )
    result = jnp.dot(flattened, w_out, preferred_element_type=jnp.float32)
    return lax.psum_scatter(
        result.reshape(
            lax.axis_size("head") * (branch_rows // head_count), 2, w_out.shape[1]
        ).astype(jnp.bfloat16),
        "head",
        scatter_dimension=0,
        tiled=True,
    )


def solution(mesh):
    return jax.shard_map(
        local,
        mesh=mesh,
        in_specs=(
            P(("groups", "branch"), None, "head", None),
            P(("groups", "branch"), None, None),
            P(("groups", "branch", "seq"), None, None),
            P("groups", None),
            P("groups"),
            P("groups"),
            P("head", None, None),
            P("head", "seq"),
        ),
        out_specs=P(("groups", "branch", "head"), None, "seq"),
        check_vma=False,
    )
```

profile of v0, /device:TPU:0, one launch (start us, length us, event | category | flops | bytes accessed | tf_op | source)
XLA Modules:
  0.0 643.1 jit_solution(3803789754475047115)
XLA Ops:
  0.0 0.0 copy-start
  0.0 0.8 reshape.264
  0.8 0.1 eq.73
  0.9 0.3 compare_reduce_fusion
  1.2 0.2 reduce_window_sum.18
  1.5 14.1 %copy.31 = bf16[64,128,576]{2,1,0:T(8,128)(2,1)} copy(bf16[64,128,576]{1,2,0:T(8,128)(2,1)} %param.10) | data formatting | bytes 18874368 | tf_op args[2]
  15.5 15.3 %reshape.265 = bf16[64,73728]{1,0:T(8,128)(2,1)} reshape(bf16[64,128,576]{2,1,0:T(8,128)(2,1)} %copy.31) | data formatting | bytes 18874368 | tf_op jit(solution)/shard_map/reshape | solution.py:67
  30.8 15.4 %dot_general.28 = bf16[128,576,64]{1,0,2:T(8,128)(2,1)} reshape(bf16[73728,64]{0,1:T(8,128)(2,1)} %bitcast.86) | data formatting | bytes 18874368 | tf_op jit(solution)/shard_map/qtk,kx->qtx/dot_general | solution.py:75
  46.2 14.6 %copy.32 = bf16[128,576,64]{0,2,1:T(8,128)(2,1)} copy(bf16[128,576,64]{1,0,2:T(8,128)(2,1)} %dot_general.28) | data formatting | bytes 18874368 | tf_op jit(solution)/shard_map/qtk,kx->qtx/dot_general | solution.py:75
  60.9 12.8 %fusion.8 = bf16[8,16,128,576]{2,1,3,0:T(8,128)(2,1)} fusion(bf16[128,576,64]{0,2,1:T(8,128)(2,1)} %copy.32, s32[8,64]{1,0:T(8,128)S(1)} %broadcast_add_fusion.2, pred[8,64]{1,0:T(8,128)(4,1)S(1)} %compare_reduce_fusion), kind=kOutput, calls=%fused_computation.12 | convolution fusion | flops 1207975936 | bytes 28314112 | tf_op jit(solution)/shard_map/qtk,kx->qtx/dot_general | solution.py:75
  73.7 0.0 copy-start.4
  73.7 0.0 copy-start.2
  73.7 0.0 copy-start.3
  73.7 0.0 copy-start.5
  73.7 6.5 %all-to-all-start = ((bf16[8,16,128,576]{2,1,3,0:T(8,128)(2,1)}), bf16[8,16,128,576]{2,1,3,0:T(8,128)(2,1)}, u32[]{:S(2)}, u32[]{:S(2)}) async-start(bf16[8,16,128,576]{2,1,3,0:T(8,128)(2,1)} %fusion.8), calls=%async_computation | async-start | bytes 37748736 | tf_op jit(solution)/shard_map/all_to_all | solution.py:82
  80.1 0.8 dynamic_slice.32
  80.9 0.1 reshape.263
  81.0 0.1 iota_add_fusion
  81.1 0.3 compare_reduce_fusion.1
  81.4 0.2 reduce_window_sum.17
  81.6 0.2 select_reduce_fusion.1
  81.9 0.1 sub.56
  81.9 0.0 copy-done.4
  82.0 0.1 dynamic_slice.33
  82.0 0.0 copy-done.2
  82.0 412.0 %all_gather.17 = bf16[16,2,576]{2,1,0:T(2,128)(2,1)S(1)} all-gather(bf16[4,2,576]{2,1,0:T(2,128)(2,1)S(1)} %copy-done.2), channel_id=1, replica_groups=mesh['groups'=2,'branch'=4,'head'=2,'seq'=2] {'branch'}, dimensions={0}, use_global_device_ids=true | all-gather | bytes 46080 | tf_op jit(solution)/shard_map/all_gather | solution.py:105
  494.1 0.0 copy-done.3
  494.1 0.1 broadcast_compare_fusion
  494.2 0.6 gather_fusion
  494.8 0.0 copy-done.5
  494.8 0.6 dynamic-slice
  496.0 0.1 broadcast_in_dim.122
  496.1 0.1 add_and_fusion
  496.2 0.1 select_reduce_fusion
  496.4 0.1 broadcast_select_fusion
  496.5 0.1 broadcast_bitcast_fusion.1
  496.6 0.1 broadcast_bitcast_fusion
  496.7 0.0 copy-done
  496.7 0.4 fusion.61
  497.1 0.3 fusion.32
  497.4 0.0 all-to-all-done
  497.4 18.4 %copy.33 = bf16[8,16,128,576]{2,1,0,3:T(8,128)(2,1)} copy(bf16[8,16,128,576]{2,1,3,0:T(8,128)(2,1)} %all-to-all-done) | data formatting | bytes 37748736 | tf_op jit(solution)/shard_map/all_to_all | solution.py:82
  515.8 28.3 %reshape.305 = bf16[16384,576,1,1]{0,1,2,3:T(8,128)(2,1)} reshape(bf16[8,16,128,576]{2,1,0,3:T(8,128)(2,1)} %copy.33) | data formatting | bytes 37748736 | tf_op jit(solution)/shard_map/reshape | solution.py:88
  544.2 17.9 %fusion.60 = (f32[4,2,32]{2,1,0:T(2,128)S(1)}, f32[4,2,32,16384]{3,2,1,0:T(8,128)}) fusion(bf16[4,2,32,576]{3,2,1,0:T(8,128)(2,1)S(1)} %copy-done, bf16[16384,576,1,1]{0,1,2,3:T(8,128)(2,1)} %reshape.305, pred[4,16384]{1,0:T(4,128)(4,1)S(1)} %fusion.32), kind=kOutput, calls=%fused_computation.96 | convolution fusion | flops 4844421120 | bytes 36013056 | tf_op jit(solution)/shard_map/rtha,ka->rthk/dot_general | solution.py:117
  562.1 9.4 %fusion.6 = f32[4,2,32]{2,1,0:T(2,128)S(1)} fusion(f32[4,2,32,16384]{3,2,1,0:T(8,128)} %get-tuple-element.40, f32[4,2,32]{2,1,0:T(2,128)S(1)} %get-tuple-element.20, pred[4,16384]{1,0:T(4,128)(4,1)S(1)} %fusion.32), kind=kLoop, calls=%fused_computation.10 | loop fusion | flops 12582656 | bytes 16844800 | tf_op jit(solution)/shard_map/reduce_sum | solution.py:129
  571.5 0.1 fusion.46
  571.6 1.8 all-gather.2
  573.4 2.0 all-gather.1
  575.4 28.2 %copy.45 = bf16[8,16,128,576]{3,2,1,0:T(8,128)(2,1)} copy(bf16[8,16,128,576]{2,1,3,0:T(8,128)(2,1)} %all-to-all-done) | data formatting | bytes 37748736 | tf_op jit(solution)/shard_map/reshape | solution.py:88
  603.6 0.0 copy-start.1
  603.6 15.1 %fusion.3 = f32[4,2,32,512]{3,2,1,0:T(8,128)S(1)} fusion(bf16[16384,576]{1,0:T(8,128)(2,1)} %bitcast.87, f32[4,2,32,16384]{3,2,1,0:T(8,128)} %get-tuple-element.40, f32[4,2,32]{2,1,0:T(2,128)S(1)} %get-tuple-element.20, pred[4,16384]{1,0:T(4,128)(4,1)S(1)} %fusion.32), kind=kOutput, calls=%fused_computation.6 | convolution fusion | flops 4307550208 | bytes 34145280 | tf_op jit(solution)/shard_map/rthk,kc->rthc/dot_general | solution.py:130
  618.8 0.4 fusion.19
  619.2 2.2 all-gather
  621.4 0.2 fusion.30
  621.6 4.4 fusion.23
  625.9 7.3 %fusion.16 = bf16[4,2,1792]{2,0,1:T(4,128)(2,1)S(1)} fusion(bf16[4096,1792]{1,0:T(8,128)(2,1)} %param.15, bf16[32,2,1,4,128]{4,3,2,1,0:T(4,128)(2,1)S(1)} %fusion.23), kind=kOutput, calls=%fused_computation.19 | convolution fusion | flops 117454848 | bytes 14774272 | tf_op jit(solution)/shard_map/dot_general | solution.py:151
  633.2 9.3 %all-reduce = bf16[4,2,1792]{2,0,1:T(4,128)(2,1)S(1)} all-reduce(bf16[4,2,1792]{2,0,1:T(4,128)(2,1)S(1)} %fusion.16), channel_id=5, replica_groups=mesh['groups'=2,'branch'=4,'head'=2,'seq'=2] {'head'}, use_global_device_ids=true, to_apply=%region_10.11.clone | all-reduce | flops 14336 | bytes 57344
  642.5 0.6 copy.38
  643.1 0.0 copy-done.1
  (20 shorter events, 0.1 us)
Async XLA Ops:
  0.0 496.7 %copy-start = (bf16[4,2,32,576]{3,2,1,0:T(8,128)(2,1)S(1)}, bf16[4,2,32,576]{3,2,1,0:T(8,128)(2,1)}, u32[]{:S(2)}) copy-start(bf16[4,2,32,576]{3,2,1,0:T(8,128)(2,1)} %param.8) | copy-start | bytes 884740
  73.7 8.3 %copy-start.4 = (s32[16]{0:T(128)S(1)}, s32[16]{0:T(128)}, u32[]{:S(2)}) copy-start(s32[16]{0:T(128)} %param.12) | copy-start | bytes 196
  73.7 8.4 %copy-start.2 = (bf16[4,2,576]{2,1,0:T(2,128)(2,1)S(1)}, bf16[4,2,576]{2,1,0:T(2,128)(2,1)}, u32[]{:S(2)}) copy-start(bf16[4,2,576]{2,1,0:T(2,128)(2,1)} %param.9) | copy-start | bytes 27652
  73.7 420.4 %copy-start.3 = (s32[16]{0:T(128)S(1)}, s32[16]{0:T(128)}, u32[]{:S(2)}) copy-start(s32[16]{0:T(128)} %param.13) | copy-start | bytes 196
  73.7 421.1 %copy-start.5 = (u32[32]{0:T(128)S(1)}, u32[32]{0:T(128)}, u32[]{:S(2)}) copy-start(u32[32]{0:T(128)} %constant.96) | copy-start | bytes 388
  73.7 423.7 %all-to-all-start = ((bf16[8,16,128,576]{2,1,3,0:T(8,128)(2,1)}), bf16[8,16,128,576]{2,1,3,0:T(8,128)(2,1)}, u32[]{:S(2)}, u32[]{:S(2)}) async-start(bf16[8,16,128,576]{2,1,3,0:T(8,128)(2,1)} %fusion.8), calls=%async_computation | async-start | bytes 37748736 | tf_op jit(solution)/shard_map/all_to_all | solution.py:82
  603.6 39.5 %copy-start.1 = (bf16[4,2,32,576]{3,2,1,0:T(8,128)(2,1)S(1)}, bf16[4,2,32,576]{3,2,1,0:T(8,128)(2,1)}, u32[]{:S(2)}) copy-start(bf16[4,2,32,576]{3,2,1,0:T(8,128)(2,1)} %param.8) | copy-start | bytes 884740
where the time goes:
time: 646 us; the launch traced here: 643 us
  blocking collectives  427 us (66%)
  local copies, waits for them, and re-layouts  138 us (21%)
  matrix products  58.2 us (9%)
  other arithmetic  11.8 us (2%)
  starting transfers between devices  6.47 us (1%)
    all_gather x1, blocking collectives, local(): everyone = lax.all_gather(kv_new, 'branch', axis=0, tiled=True)  412 us
    reshape x2, local copies, waits for them, and re-layouts, local(): key_rows = arrived.reshape(-1, feature)  56.6 us
    dot_general x2, local copies, waits for them, and re-layouts, local(): jnp.einsum('qtk,kx->qtx', outgoing.astype(jnp.bfloat16), flat_cache, pref...  30.1 us
    all_to_all x1, local copies, waits for them, and re-layouts, local(): lax.all_to_all(buffer, ('branch', 'seq'), split_axis=0, concat_axis=0, ti...  18.4 us
    dot_general x1, matrix products, local(): jnp.einsum('rtha,ka->rthk', queries, key_rows, preferred_element_type=jnp...  17.9 us
    reshape x1, local copies, waits for them, and re-layouts, local(): flat_cache = cache.reshape(block_count, block_len * feature)  15.3 us
    dot_general x1, matrix products, local(): jnp.einsum('rthk,kc->rthc', exps.astype(jnp.bfloat16), key_rows[:, :laten...  15.1 us
    unnamed x17, local copies, waits for them, and re-layouts  14.9 us
  transfers between devices with their start and end apart: 1, of which 0 were waited for; matrix products, arithmetic and copies ran while one was open for 1% of the time, Pallas kernels for 0%

commit v1 on v0

v1 whole, which is shorter than its diff:
```python
import jax
import jax.numpy as jnp
from jax import lax
from jax.sharding import PartitionSpec as P

ROPE = 64
VHEAD = 128


def slots_of(block_list, lengths, my_index, block_count, block_len, rows, slots):
    mine = block_list - my_index * block_count
    lead = mine[::rows]
    held = (lead >= 0) & (lead < block_count)
    spots = jnp.arange(mine.shape[1])
    before = spots[None, :] < spots[:, None]
    rank = jnp.sum((held[:, None, :] & before[None]).astype(jnp.int32), axis=2)
    slot = jnp.arange(slots)
    chosen = held[:, None, :] & (rank[:, None, :] == slot[None, :, None])
    ids = jnp.sum(jnp.where(chosen, lead[:, None, :], 0), axis=2)
    all_ids = jnp.repeat(ids, rows, axis=0)
    match = mine[:, None, :] == all_ids[:, :, None]
    place = jnp.sum(jnp.where(match, spots, 0), axis=2)
    room = lengths[:, None] - place * block_len
    bias = jnp.where(jnp.arange(block_len) < room[:, :, None], 0.0, -1e30)
    return ids, bias.reshape(mine.shape[0], slots * block_len)


def local(queries, kv_new, cache, block_list, lengths, parent, w_uv, w_out):
    rows, _, heads, feature = queries.shape
    block_count, block_len, _ = cache.shape
    latent = w_uv.shape[1]
    branch_count = lax.axis_size("branch")
    seq_count = lax.axis_size("seq")
    head_count = lax.axis_size("head")
    branch_at = lax.axis_index("branch")
    my_index = branch_at * seq_count + lax.axis_index("seq")
    slots = block_list.shape[1] // (branch_count * seq_count)
    scale = float(VHEAD + ROPE) ** (-0.5) * 1.4426950408889634
    ids, bias = slots_of(block_list, lengths, my_index, block_count, block_len, rows, slots)
    everyone = lax.all_gather(queries, "branch", axis=0)
    keys = jnp.take(cache, ids.reshape(-1), axis=0).reshape(branch_count, slots * block_len, feature)
    scores = jnp.einsum(
        "brtha,bka->brthk", everyone, keys, preferred_element_type=jnp.float32
    ) * scale
    scores = scores + bias.reshape(branch_count, rows, 1, 1, -1)
    peak = jnp.max(scores, axis=-1)
    exps = jnp.exp2(scores - peak[..., None])
    totals = jnp.sum(exps, axis=-1)
    summed = jnp.einsum(
        "brthk,bkc->brthc",
        exps.astype(jnp.bfloat16),
        keys[:, :, :latent],
        preferred_element_type=jnp.float32,
    ).astype(jnp.bfloat16)
    stats = jnp.stack([peak, totals], axis=1)
    summed = lax.all_to_all(summed, "branch", 0, 0, tiled=True)
    stats = lax.all_to_all(stats, "branch", 0, 0, tiled=True)
    summed = lax.all_gather(summed, "seq", axis=0, tiled=True)
    stats = lax.all_gather(stats, "seq", axis=0, tiled=True)
    new_keys = lax.all_gather(kv_new, "branch", axis=0, tiled=True)
    parents = lax.dynamic_slice_in_dim(parent, branch_at * rows, rows)
    own = branch_at * rows + jnp.arange(rows)
    which = jnp.arange(new_keys.shape[0])
    draft = jnp.arange(2)
    seen = (which[None, :] == parents[:, None])[:, None, :, None] | (
        (which[None, :] == own[:, None])[:, None, :, None]
        & (draft[None, :] <= draft[:, None])[None, :, None, :]
    )
    new_scores = jnp.einsum(
        "rtha,bua->rthbu", queries, new_keys, preferred_element_type=jnp.float32
    ) * scale
    new_scores = jnp.where(seen[:, :, None], new_scores, -1e30)
    new_scores = new_scores.reshape(rows, 2, heads, -1)
    top = jnp.maximum(jnp.max(stats[:, 0], axis=0), jnp.max(new_scores, axis=-1))
    new_exps = jnp.exp2(new_scores - top[..., None])
    part = jnp.exp2(stats[:, 0] - top[None])
    total = jnp.sum(part * stats[:, 1], axis=0) + jnp.sum(new_exps, axis=-1)
    latent_out = jnp.sum(part[..., None] * summed.astype(jnp.float32), axis=0) + jnp.einsum(
        "rthk,kc->rthc",
        new_exps.astype(jnp.bfloat16),
        new_keys.reshape(-1, feature)[:, :latent],
        preferred_element_type=jnp.float32,
    )
    latent_out = latent_out / total[..., None]
    head_out = jnp.einsum(
        "rthc,hcv->rthv",
        latent_out,
        w_uv.astype(jnp.float32),
        precision=lax.Precision.HIGHEST,
    ).astype(jnp.bfloat16)
    result = jnp.dot(
        head_out.reshape(rows * 2, -1), w_out, preferred_element_type=jnp.float32
    )
    return lax.psum_scatter(
        result.reshape(rows, 2, w_out.shape[1]).astype(jnp.bfloat16),
        "head",
        scatter_dimension=0,
        tiled=True,
    )


def solution(mesh):
    return jax.shard_map(
        local,
        mesh=mesh,
        in_specs=(
            P(("groups", "branch"), None, "head", None),
            P(("groups", "branch"), None, None),
            P(("groups", "branch", "seq"), None, None),
            P("groups", None),
            P("groups"),
            P("groups"),
            P("head", None, None),
            P("head", "seq"),
        ),
        out_specs=P(("groups", "branch", "head"), None, "seq"),
        check_vma=False,
    )
```

time: 646 us -> 152 us (0.24)
  blocking collectives: 427 us -> 41.6 us
  local copies, waits for them, and re-layouts: 138 us -> 28 us
  matrix products: 58.2 us -> 32.8 us
  between operations: 0.86 us -> 14.2 us
  other arithmetic: 11.8 us -> 19.9 us
    all_gather x4 -> x2, blocking collectives: 418 us -> 33.3 us  [the longest x1 31.2 us: local(): new_keys = lax.all_gather(kv_new, 'branch', axis=0, tiled=True)]
    reshape x6 -> x2, local copies, waits for them, and re-layouts: 72.8 us -> 0.13 us  [the longest x1 0.09 us: local(): ids.reshape(-1)]
    dot_general x2 -> x0, local copies, waits for them, and re-layouts: 30.1 us -> none  [local(): jnp.einsum('qtk,kx->qtx', outgoing.astype(jnp.bfloat16), flat_cache, pref...]
    dot_general x7 -> x6, matrix products: 58.2 us -> 32.8 us  [the longest x1 11.2 us: local(): jnp.einsum('brtha,bka->brthk', everyone, keys, preferred_element_type=jnp...]
    gather x1 -> x2, local copies, waits for them, and re-layouts: 0.58 us -> 23.9 us  [local(): jnp.take(cache, ids.reshape(-1), axis=0)]
    all_to_all x1 -> x2, local copies, waits for them, and re-layouts: 18.4 us -> 0.52 us  [local(): stats = lax.all_to_all(stats, 'branch', 0, 0, tiled=True)]
    unnamed x17 -> x18, local copies, waits for them, and re-layouts: 14.9 us -> 2.46 us
    select_n x1 -> x3, other arithmetic: 0.08 us -> 10.7 us  [the longest x2 10.7 us: local(): jnp.take(cache, ids.reshape(-1), axis=0)]
  transfers between devices with their start and end apart: 1 -> 4, of which waited for: 0 -> 2; matrix products, arithmetic and copies ran while one was open for 1% -> 29% of each run, Pallas kernels for 0% -> 0%
where the time goes in v1:
time: 152 us; the launch traced here: 151 us
  blocking collectives  41.6 us (27%)
  matrix products  32.8 us (22%)
  local copies, waits for them, and re-layouts  28 us (18%)
  other arithmetic  19.9 us (13%)
  between operations  14.2 us (9%)
  starting transfers between devices  9.73 us (6%)
  waiting for transfers between devices  5.13 us (3%)
    all_gather x1, blocking collectives, local(): new_keys = lax.all_gather(kv_new, 'branch', axis=0, tiled=True)  31.2 us
    gather x2, local copies, waits for them, and re-layouts, local(): jnp.take(cache, ids.reshape(-1), axis=0)  23.9 us
    dot_general x1, matrix products, local(): jnp.einsum('brtha,bka->brthk', everyone, keys, preferred_element_type=jnp...  11.2 us
    select_n x2, other arithmetic, local(): jnp.take(cache, ids.reshape(-1), axis=0)  10.7 us
    dot_general x1, matrix products, local(): jnp.einsum('brthk,bkc->brthc', exps.astype(jnp.bfloat16), keys[:, :, :lat...  9.26 us
    unnamed x1, blocking collectives  8.35 us
    dot_general x1, matrix products, local(): jnp.dot(head_out.reshape(rows * 2, -1), w_out, preferred_element_type=jnp...  7.28 us
    all_to_all x1, starting transfers between devices, local(): summed = lax.all_to_all(summed, 'branch', 0, 0, tiled=True)  5.97 us
  transfers between devices with their start and end apart: 4, of which 2 were waited for; matrix products, arithmetic and copies ran while one was open for 29% of the time, Pallas kernels for 0%

profile of v1, /device:TPU:0, one launch (start us, length us, event | category | flops | bytes accessed | tf_op | source)
XLA Modules:
  0.0 151.3 jit_solution(17880979031699706780)
XLA Ops:
  6.5 0.0 all-gather.6.cloned.1.call-start
  6.5 0.7 all-gather.6.cloned.1.call-update
  7.3 0.7 broadcast_subtract_fusion
  8.0 0.1 convert_reduce_fusion
  8.2 0.1 select_reduce_fusion.1
  8.3 0.1 reshape.178
  8.5 9.8 %gather_fusion = bf16[64,128,576]{1,2,0:T(8,128)(2,1)} fusion(bf16[64,128,576]{1,2,0:T(8,128)(2,1)} %param.10, s32[1024]{0:T(1024)S(1)} %pad_clamp_fusion), kind=kCustom, calls=%fused_computation | custom fusion | bytes 18874624 | tf_op jit(solution)/shard_map/jit(_take)/gather | solution.py:41
  18.3 0.0 copy-start.3
  18.3 14.1 %copy.102 = bf16[64,128,576]{2,1,0:T(8,128)(2,1)} copy(bf16[64,128,576]{1,2,0:T(8,128)(2,1)} %gather_fusion) | data formatting | bytes 18874368 | tf_op jit(solution)/shard_map/jit(_take)/gather | solution.py:41
  32.4 0.1 broadcast_bitcast_fusion
  32.5 0.4 select_reduce_fusion
  32.9 0.0 copy-done.3
  32.9 0.1 multiply_subtract_fusion
  33.0 0.1 lt.83
  33.2 10.7 %bitcast_select_fusion = bf16[4,2048,576]{2,1,0:T(8,128)(2,1)} fusion(pred[4,2048]{1,0:T(4,128)(4,1)S(1)} %bitcast.101, bf16[4,2048,576]{2,1,0:T(8,128)(2,1)} %bitcast.95), kind=kLoop, calls=%fused_computation.5 | loop fusion | flops 4718592 | bytes 18882560 | tf_op jit(solution)/shard_map/jit(_take)/select_n | solution.py:41
  43.9 0.5 all-gather.6.cloned.1.call-done
  44.4 11.2 %fusion.5 = (f32[4,4,2,32]{3,2,1,0:T(2,128)S(1)}, f32[4,2048,4,2,32]{1,4,3,2,0:T(8,128)}) fusion(f32[4,4,2048]{2,1,0:T(4,128)S(1)} %compare_select_fusion, bf16[4,4,2,32,576]{4,3,2,1,0:T(8,128)(2,1)} %bitcast.96, bf16[4,2048,576]{2,1,0:T(8,128)(2,1)} %bitcast_select_fusion), kind=kOutput, calls=%fused_computation.10 | convolution fusion | flops 2422209536 | bytes 19140608 | tf_op jit(solution)/shard_map/brtha,bka->brthk/dot_general | solution.py:42
  55.5 0.0 copy-start.4
  55.5 0.0 copy-start.2
  55.5 9.3 %fusion.18 = bf16[4,4,2,32,512]{4,3,2,1,0:T(8,128)(2,1)} fusion(bf16[4,2048,576]{2,1,0:T(8,128)(2,1)} %bitcast_select_fusion, f32[4,2048,4,2,32]{1,4,3,2,0:T(8,128)} %get-tuple-element.8, f32[4,4,2,32]{3,2,1,0:T(2,128)S(1)} %get-tuple-element.7, f32[4,4,2048]{2,1,0:T(4,128)S(1)} %compare_select_fusion), kind=kOutput, calls=%fused_computation.21 | convolution fusion | flops 2158493696 | bytes 17960960 | tf_op jit(solution)/shard_map/brthk,bkc->brthc/dot_general | solution.py:49
  64.8 0.0 copy-start.1
  64.8 0.0 copy-start.5
  64.8 6.0 %all-to-all-start.1 = ((bf16[4,4,2,32,512]{4,3,2,1,0:T(8,128)(2,1)}), bf16[4,4,2,32,512]{4,3,2,1,0:T(8,128)(2,1)S(1)}, u32[]{:S(2)}, u32[]{:S(2)}) async-start(bf16[4,4,2,32,512]{4,3,2,1,0:T(8,128)(2,1)} %fusion.18), calls=%async_computation.1 | async-start | bytes 2097152 | tf_op jit(solution)/shard_map/all_to_all | solution.py:56
  70.8 0.0 all-gather.4.cloned.1.call-start
  70.8 0.0 copy-done.4
  70.8 0.1 dynamic_slice.3
  70.8 0.0 copy-done.2
  70.8 31.2 %all_gather.18 = bf16[16,2,576]{2,1,0:T(2,128)(2,1)S(1)} all-gather(bf16[4,2,576]{2,1,0:T(2,128)(2,1)S(1)} %copy-done.2), channel_id=1, replica_groups=mesh['groups'=2,'branch'=4,'head'=2,'seq'=2] {'branch'}, dimensions={0}, use_global_device_ids=true | all-gather | bytes 46080 | tf_op jit(solution)/shard_map/all_gather | solution.py:60
  102.1 0.1 iota_compare_fusion.2
  102.2 0.0 all-to-all-done.1
  102.2 0.0 copy-start
  102.2 1.0 copy-done
  103.2 0.0 all-gather.4.cloned.1.call-update
  103.2 0.1 and_or_fusion
  103.3 4.6 %fusion.7 = f32[4,4,2,32]{3,2,1,0:T(2,128)S(1)} fusion(f32[4,2048,4,2,32]{1,4,3,2,0:T(8,128)} %get-tuple-element.8, f32[4,4,2,32]{3,2,1,0:T(2,128)S(1)} %get-tuple-element.7, f32[4,4,2048]{2,1,0:T(4,128)S(1)} %compare_select_fusion), kind=kLoop, calls=%fused_computation.12 | loop fusion | flops 10484736 | bytes 8527872 | tf_op jit(solution)/shard_map/reduce_sum | solution.py:48
  107.8 0.7 reshape.201
  108.5 3.8 %all-to-all-start = ((f32[4,1,512]{2,1,0:T(1,128)}), f32[4,1,512]{2,1,0:T(1,128)S(1)}, u32[]{:S(2)}, u32[]{:S(2)}) async-start(f32[4,1,512]{2,1,0:T(1,128)} %reshape.201), calls=%async_computation | async-start | bytes 16384 | tf_op jit(solution)/shard_map/all_to_all | solution.py:57
  112.3 0.0 copy-done.1
  112.3 0.4 fusion.46
  112.8 0.1 copy.86
  112.9 0.0 copy-done.5
  112.9 0.6 dynamic-slice
  114.0 3.9 %all-to-all-done = f32[4,1,512]{2,1,0:T(1,128)S(1)} async-done(((f32[4,1,512]{2,1,0:T(1,128)}), f32[4,1,512]{2,1,0:T(1,128)S(1)}, u32[]{:S(2)}, u32[]{:S(2)}) %all-to-all-start) | async-done | bytes 8224 | tf_op jit(solution)/shard_map/all_to_all | solution.py:57
  117.9 0.5 broadcast.137
  118.4 0.7 reduce.3
  119.1 0.1 reshape.202
  119.2 2.0 %all_gather.17 = f32[8,2,4,2,32]{4,2,3,1,0:T(4,128)S(1)} all-gather(f32[4,2,4,2,32]{4,2,3,1,0:T(4,128)S(1)} %copy.81), channel_id=1, replica_groups=mesh['groups'=2,'branch'=4,'head'=2,'seq'=2] {'seq'}, dimensions={0}, use_global_device_ids=true | all-gather | bytes 24576 | tf_op jit(solution)/shard_map/all_gather | solution.py:59
  121.4 0.0 all-gather.4.cloned.1.call-done
  121.4 2.1 %multiply_reduce_fusion = f32[4,2,32,512]{3,2,1,0:T(8,128)S(1)} fusion(bf16[8,4,2,32,512]{4,3,2,1,0:T(8,128)(2,1)} %all-gather.4.cloned.1.call-done, f32[8,4,2,32]{3,2,1,0:T(2,128)S(1)} %copy.85), kind=kLoop, calls=%fused_computation.15 | loop fusion | flops 3014656 | bytes 2629632 | tf_op jit(solution)/shard_map/reduce_sum | solution.py:78
  123.5 0.3 fusion.21
  123.8 4.4 %fusion.26 = bf16[32,2,1,4,128]{4,3,2,1,0:T(4,128)(2,1)S(1)} fusion(bf16[32,512,128]{2,1,0:T(8,128)(2,1)} %param.14, f32[4,2,32,512]{3,2,1,0:T(8,128)S(1)} %fusion.21), kind=kOutput, calls=%fused_computation.27 | convolution fusion | flops 201359360 | bytes 4784128 | tf_op jit(solution)/shard_map/rthc,hcv->rthv/dot_general | solution.py:85
  128.2 7.3 %fusion.15 = bf16[4,2,1792]{2,0,1:T(4,128)(2,1)S(1)} fusion(bf16[4096,1792]{1,0:T(8,128)(2,1)} %param.15, bf16[32,2,1,4,128]{4,3,2,1,0:T(4,128)(2,1)S(1)} %fusion.26), kind=kOutput, calls=%fused_computation.20 | convolution fusion | flops 117454848 | bytes 14774272 | tf_op jit(solution)/shard_map/dot_general | solution.py:91
  135.5 8.3 %all-reduce = bf16[4,2,1792]{2,0,1:T(4,128)(2,1)S(1)} all-reduce(bf16[4,2,1792]{2,0,1:T(4,128)(2,1)S(1)} %fusion.15), channel_id=3, replica_groups=mesh['groups'=2,'branch'=4,'head'=2,'seq'=2] {'head'}, use_global_device_ids=true, to_apply=%region_10.11.clone | all-reduce | flops 14336 | bytes 57344
  143.8 0.6 copy.94
  (24 shorter events, 0.4 us)
Async XLA Ops:
  6.5 37.8 %all-gather.6.cloned.1.call-start = ((), (), s32[]{:S(2)}) async-start(), calls=%async_computation.3 | async-start | bytes 1638400 | tf_op jit(solution)/shard_map/all_gather | solution.py:40
  18.3 14.6 %copy-start.3 = (s32[16]{0:T(128)S(1)}, s32[16]{0:T(128)}, u32[]{:S(2)}) copy-start(s32[16]{0:T(128)} %param.12) | copy-start | bytes 196
  55.5 15.3 %copy-start.4 = (s32[16]{0:T(128)S(1)}, s32[16]{0:T(128)}, u32[]{:S(2)}) copy-start(s32[16]{0:T(128)} %param.13) | copy-start | bytes 196
  55.5 15.3 %copy-start.2 = (bf16[4,2,576]{2,1,0:T(2,128)(2,1)S(1)}, bf16[4,2,576]{2,1,0:T(2,128)(2,1)}, u32[]{:S(2)}) copy-start(bf16[4,2,576]{2,1,0:T(2,128)(2,1)} %param.9) | copy-start | bytes 27652
  64.8 47.5 %copy-start.1 = (bf16[4,2,32,576]{3,2,1,0:T(8,128)(2,1)S(1)}, bf16[4,2,32,576]{3,2,1,0:T(8,128)(2,1)}, u32[]{:S(2)}) copy-start(bf16[4,2,32,576]{3,2,1,0:T(8,128)(2,1)} %param.8) | copy-start | bytes 884740
  64.8 48.1 %copy-start.5 = (u32[32]{0:T(128)S(1)}, u32[32]{0:T(128)}, u32[]{:S(2)}) copy-start(u32[32]{0:T(128)} %constant.54) | copy-start | bytes 388
  64.8 37.4 %all-to-all-start.1 = ((bf16[4,4,2,32,512]{4,3,2,1,0:T(8,128)(2,1)}), bf16[4,4,2,32,512]{4,3,2,1,0:T(8,128)(2,1)S(1)}, u32[]{:S(2)}, u32[]{:S(2)}) async-start(bf16[4,4,2,32,512]{4,3,2,1,0:T(8,128)(2,1)} %fusion.18), calls=%async_computation.1 | async-start | bytes 2097152 | tf_op jit(solution)/shard_map/all_to_all | solution.py:56
  70.8 50.7 %all-gather.4.cloned.1.call-start = ((), (), s32[]{:S(2)}) async-start(), calls=%async_computation.2 | async-start | bytes 3145728 | tf_op jit(solution)/shard_map/all_gather | solution.py:58
  102.2 1.0 copy-start
  108.5 9.3 %all-to-all-start = ((f32[4,1,512]{2,1,0:T(1,128)}), f32[4,1,512]{2,1,0:T(1,128)S(1)}, u32[]{:S(2)}, u32[]{:S(2)}) async-start(f32[4,1,512]{2,1,0:T(1,128)} %reshape.201), calls=%async_computation | async-start | bytes 16384 | tf_op jit(solution)/shard_map/all_to_all | solution.py:57
Sparse Core Ops, SparseCore 0:
  8.9 35.3 all-gather.5
  103.3 10.7 all-gather.3

commit v2 on v1

v2 whole, which is shorter than its diff:
```python
import functools

import jax
import jax.numpy as jnp
from jax import lax
from jax.experimental import pallas as pl
from jax.experimental.pallas import tpu as pltpu
from jax.sharding import PartitionSpec as P

ROPE = 64
VHEAD = 128
MESH = pl.DeviceIdType.MESH
LOW = -1e30


def slots_of(block_list, lengths, my_index, block_count, block_len, rows, slots):
    mine = block_list - my_index * block_count
    lead = mine[::rows]
    held = (lead >= 0) & (lead < block_count)
    spots = jnp.arange(mine.shape[1])
    before = spots[None, :] < spots[:, None]
    rank = jnp.sum((held[:, None, :] & before[None]).astype(jnp.int32), axis=2)
    slot = jnp.arange(slots)
    chosen = held[:, None, :] & (rank[:, None, :] == slot[None, :, None])
    ids = jnp.sum(jnp.where(chosen, lead[:, None, :], 0), axis=2)
    all_ids = jnp.repeat(ids, rows, axis=0)
    match = mine[:, None, :] == all_ids[:, :, None]
    place = jnp.sum(jnp.where(match, spots, 0), axis=2)
    room = lengths[:, None] - place * block_len
    bias = jnp.where(jnp.arange(block_len) < room[:, :, None], 0.0, LOW)
    return ids, bias.reshape(-1, rows, slots * block_len)


def as_row(column):
    short = 128 - column.shape[0]
    if short > 0:
        column = jnp.concatenate([column, jnp.zeros((short, 128), jnp.float32)], axis=0)
    return jnp.transpose(column)[:8]


def as_columns(rows_in, height):
    lane = lax.broadcasted_iota(jnp.int32, (128, rows_in[0].shape[1]), 0)
    stacked = jnp.zeros(lane.shape, jnp.float32)
    for j, row in enumerate(rows_in):
        stacked = jnp.where(lane == j, row[0:1], stacked)
    return jnp.transpose(stacked)[:height]


def pair_row(peak, total):
    lane = lax.broadcasted_iota(jnp.int32, (peak.shape[0], 128), 1)
    return as_row(jnp.where(lane == 0, peak, total))


def kernel(
    scale,
    rows,
    ids_ref,
    bias_ref,
    new_bias_ref,
    q_ref,
    kv_ref,
    cache_ref,
    uv_ref,
    out_w_ref,
    out_ref,
    cache_v,
    uv_v,
    out_v,
    q_all,
    kv_all,
    keys,
    scores,
    probs,
    column,
    o_out,
    o_in,
    s_out,
    s_in,
    z_out,
    z_in,
    zs_out,
    zs_in,
    latent_v,
    head_v,
    red_out,
    red_in,
    local_sem,
    q_send,
    q_recv,
    f_send,
    f_recv,
    kv_send,
    kv_recv,
    o_send,
    o_recv,
    s_send,
    s_recv,
    z_send,
    z_recv,
    zs_send,
    zs_recv,
    h_send,
    h_recv,
    r_send,
    r_recv,
):
    nb, hc = lax.axis_size("branch"), lax.axis_size("head")
    z, x, core = lax.axis_index("branch"), lax.axis_index("head"), lax.axis_index("seq")
    other = 1 - core
    height, feature = q_ref.shape[1], q_ref.shape[2]
    block_len = cache_v.shape[1]
    slots = ids_ref.shape[1]
    latent = uv_v.shape[1]
    heads = uv_v.shape[0]
    groups = rows * 2

    cache_copy = pltpu.make_async_copy(cache_ref, cache_v, local_sem.at[0])
    cache_copy.start()
    uv_copy = pltpu.make_async_copy(uv_ref.at[pl.ds(core * heads, heads)], uv_v, local_sem.at[1])
    uv_copy.start()
    depth = out_v.shape[1]
    out_copies = []
    for g in range(2):
        out_copies.append(
            pltpu.make_async_copy(
                out_w_ref.at[pl.ds(g * depth, depth)], out_v.at[g], local_sem.at[2 + g]
            )
        )
        out_copies[-1].start()

    barrier = pltpu.get_barrier_semaphore()
    for d in range(1, nb):
        pl.semaphore_signal(
            barrier, inc=1, device_id={"branch": lax.rem(z + d, nb)}, device_id_type=MESH
        )
    for e in range(1, hc):
        pl.semaphore_signal(
            barrier, inc=1, device_id={"head": lax.rem(x + e, hc)}, device_id_type=MESH
        )
    pl.semaphore_signal(barrier, inc=1, device_id={"seq": other}, device_id_type=MESH)
    pl.semaphore_wait(barrier, nb - 1 + hc - 1 + 1)

    def remote(src, dst, send, recv, target):
        return pltpu.make_async_remote_copy(
            src_ref=src,
            dst_ref=dst,
            send_sem=send,
            recv_sem=recv,
            device_id=target,
            device_id_type=MESH,
        )

    sent = []

    def go(copy):
        copy.start()
        sent.append(copy)
        return copy

    q_copies, kv_copies = [None], [None]
    for d in range(1, nb):
        there = {"branch": lax.rem(z + d, nb)}
        q_copies.append(
            go(remote(q_ref.at[core], q_all.at[d, core], q_send.at[d], q_recv.at[d], there))
        )
    for d in range(1, nb):
        there = {"branch": lax.rem(z + d, nb)}
        kv_copies.append(go(remote(kv_ref, kv_all.at[d], kv_send.at[d], kv_recv.at[d], there)))
    kv_all[0] = kv_ref[...]

    o_copies, s_copies, z_copies, zs_copies = [], [], [None], [None]

    def attend(d):
        source = lax.rem(z + nb - d, nb)
        for s in range(slots):
            keys[s * block_len : (s + 1) * block_len, :] = cache_v[ids_ref[source, s]]
        q = (q_ref if d == 0 else q_all.at[d])[...].reshape(2 * height, feature)
        scores[...] = lax.dot_general(
            q, keys[...], (((1,), (1,)), ((), ())), preferred_element_type=jnp.float32
        )
        size = height // rows
        for g in range(2):
            for r in range(rows):
                at = g * height + r * size
                v = scores[at : at + size, :] * scale + bias_ref[source, r : r + 1, :]
                peak = jnp.max(v, axis=1, keepdims=True)
                p = jnp.exp2(v - peak)
                total = jnp.sum(p, axis=1, keepdims=True)
                probs[at : at + size, :] = p.astype(jnp.bfloat16)
                lane = lax.broadcasted_iota(jnp.int32, (size, 128), 1)
                column[at : at + size, :] = jnp.where(lane == 0, peak, total)
        for g in range(2):
            s_out[d, g] = as_row(column[g * height : (g + 1) * height, :])
        summed = jnp.dot(probs[...], keys[:, :latent], preferred_element_type=jnp.float32)
        o_out[d] = summed.astype(jnp.bfloat16).reshape(2, height, latent)
        partner = {"seq": other}
        s_copies.append(go(remote(s_out.at[d, other], s_in.at[d], s_send.at[d], s_recv.at[d], partner)))
        o_copies.append(go(remote(o_out.at[d, other], o_in.at[d], o_send.at[d], o_recv.at[d], partner)))

    def merge(d):
        s_copies[d].wait_recv()
        one, two = s_out[d, core], s_in[d]
        top = jnp.maximum(one[0:1], two[0:1])
        c1, c2 = jnp.exp2(one[0:1] - top), jnp.exp2(two[0:1] - top)
        total = one[1:2] * c1 + two[1:2] * c2
        line = lax.broadcasted_iota(jnp.int32, zs_out.shape[1:], 0)
        zs_out[d] = jnp.where(line == 0, top, total)
        cols = as_columns([c1, c2], height)
        o_copies[d].wait_recv()
        merged = o_out[d, core].astype(jnp.float32) * cols[:, 0:1] + o_in[d].astype(
            jnp.float32
        ) * cols[:, 1:2]
        z_out[d] = merged.astype(jnp.bfloat16)
        if d > 0:
            there = {"branch": lax.rem(z + nb - d, nb)}
            zs_copies.append(
                go(remote(zs_out.at[d], zs_in.at[d], zs_send.at[d], zs_recv.at[d], there))
            )
            z_copies.append(go(remote(z_out.at[d], z_in.at[d], z_send.at[d], z_recv.at[d], there)))

    cache_copy.wait()
    forwards = [None]
    attend(0)
    for d in range(1, nb):
        q_copies[d].wait_recv()
        forward = go(
            remote(
                q_all.at[d, core], q_all.at[d, core], f_send.at[d], f_recv.at[d], {"seq": other}
            )
        )
        merge(d - 1)
        forward.wait_recv()
        attend(d)
    merge(nb - 1)

    for d in range(1, nb):
        kv_copies[d].wait_recv()
    new_keys = kv_all[...].reshape(-1, feature)
    size = height // groups
    new_scores = lax.dot_general(
        q_ref[core], new_keys, (((1,), (1,)), ((), ())), preferred_element_type=jnp.float32
    )
    new_v = new_scores.reshape(groups, size, -1) * scale + new_bias_ref[...][:, None, :]
    new_v = new_v.reshape(height, -1)
    new_peak = jnp.max(new_v, axis=1, keepdims=True)
    new_p = jnp.exp2(new_v - new_peak)
    new_total = jnp.sum(new_p, axis=1, keepdims=True)
    new_row = pair_row(new_peak, new_total)
    new_sum = jnp.dot(
        new_p.astype(jnp.bfloat16), new_keys[:, :latent], preferred_element_type=jnp.float32
    )

    stats = [zs_out[0], new_row]
    for d in range(1, nb):
        zs_copies[d].wait_recv()
        stats.append(zs_in[d])
    top = functools.reduce(jnp.maximum, [s[0:1] for s in stats])
    shares = [jnp.exp2(s[0:1] - top) for s in stats]
    total = sum(c * s[1:2] for c, s in zip(shares, stats))
    cols = as_columns([c / total for c in shares], height)
    latent_out = z_out[0].astype(jnp.float32) * cols[:, 0:1] + new_sum * cols[:, 1:2]
    for d in range(1, nb):
        z_copies[d].wait_recv()
        latent_out = latent_out + z_in[d].astype(jnp.float32) * cols[:, d + 1 : d + 2]
    for j in range(latent // 128):
        latent_v[j] = latent_out[:, j * 128 : (j + 1) * 128]

    uv_copy.wait()
    for h in range(heads):
        part = jnp.concatenate(
            [latent_v[j, pl.ds(h, groups, stride=heads), :] for j in range(latent // 128)], axis=1
        )
        high = part.astype(jnp.bfloat16)
        rest = (part - high.astype(jnp.float32)).astype(jnp.bfloat16)
        both = jnp.dot(
            jnp.concatenate([high, rest], axis=0), uv_v[h], preferred_element_type=jnp.float32
        )
        up = both[:groups] + both[groups:]
        head_v[core, :, h * VHEAD : (h + 1) * VHEAD] = jnp.concatenate([up, up], axis=0).astype(
            jnp.bfloat16
        )
    swap = go(
        remote(head_v.at[core], head_v.at[core], h_send.at[0], h_recv.at[0], {"seq": other})
    )
    for copy in out_copies:
        copy.wait()
    result = jnp.dot(head_v[core], out_v[core], preferred_element_type=jnp.float32)
    swap.wait_recv()
    result = result + jnp.dot(head_v[other], out_v[other], preferred_element_type=jnp.float32)
    result = result[:groups]
    red_out[...] = result
    reds = []
    for e in range(1, hc):
        there = {"head": lax.rem(x + e, hc)}
        reds.append(
            go(remote(red_out, red_in.at[e - 1], r_send.at[e - 1], r_recv.at[e - 1], there))
        )
    for e in range(1, hc):
        reds[e - 1].wait_recv()
        result = result + red_in[e - 1]
    count = out_ref.shape[0]
    mine = jnp.zeros(out_ref.shape, jnp.float32)
    for k in range(hc):
        mine = jnp.where(x == k, result[k * count : (k + 1) * count], mine)
    out_ref[...] = mine.astype(out_ref.dtype)
    for copy in sent:
        copy.wait_send()


def local(queries, kv_new, cache, block_list, lengths, parent, w_uv, w_out):
    rows, _, heads, feature = queries.shape
    block_count, block_len, _ = cache.shape
    latent = w_uv.shape[1]
    nb = lax.axis_size("branch")
    ns = lax.axis_size("seq")
    hc = lax.axis_size("head")
    branch_at = lax.axis_index("branch")
    my_index = branch_at * ns + lax.axis_index("seq")
    slots = block_list.shape[1] // (nb * ns)
    scale = float(VHEAD + ROPE) ** (-0.5) * 1.4426950408889634
    ids, bias = slots_of(block_list, lengths, my_index, block_count, block_len, rows, slots)
    half = heads // 2
    groups = rows * 2
    height = groups * half
    q = queries.reshape(groups, 2, half, feature).transpose(1, 0, 2, 3)
    q = q.reshape(2, height, feature)
    pad = 16
    kv = jnp.pad(kv_new.reshape(groups, feature), ((0, pad - groups), (0, 0)))

    parents = lax.dynamic_slice_in_dim(parent, branch_at * rows, rows)
    spot = jnp.arange(nb * pad)
    origin = (branch_at - spot // pad + nb) % nb
    inner = spot % pad
    which = jnp.where(inner < groups, origin * rows + inner // 2, -2)
    own = branch_at * rows + jnp.arange(rows)
    seen = (which[None, None, :] == parents[:, None, None]) | (
        (which[None, None, :] == own[:, None, None])
        & ((inner % 2)[None, None, :] <= jnp.arange(2)[None, :, None])
    )
    new_bias = jnp.where(seen, 0.0, LOW).reshape(groups, nb * pad)

    depth = w_out.shape[0] // 2
    width = w_out.shape[1]
    dma = pltpu.SemaphoreType.DMA
    vmem = pl.BlockSpec(memory_space=pltpu.VMEM)
    hbm = pl.BlockSpec(memory_space=pl.ANY)
    count = groups // hc
    bf16, f32 = jnp.bfloat16, jnp.float32
    out = pl.pallas_call(
        functools.partial(kernel, scale, rows),
        out_shape=jax.ShapeDtypeStruct((count, width), bf16),
        in_specs=[
            pl.BlockSpec(memory_space=pltpu.SMEM),
            vmem,
            vmem,
            vmem,
            vmem,
            hbm,
            hbm,
            hbm,
        ],
        out_specs=vmem,
        scratch_shapes=[
            pltpu.VMEM((block_count, block_len, feature), bf16),
            pltpu.VMEM((half, latent, VHEAD), bf16),
            pltpu.VMEM((2, depth, width), bf16),
            pltpu.VMEM((nb, 2, height, feature), bf16),
            pltpu.VMEM((nb, pad, feature), bf16),
            pltpu.VMEM((slots * block_len, feature), bf16),
            pltpu.VMEM((2 * height, slots * block_len), f32),
            pltpu.VMEM((2 * height, slots * block_len), bf16),
            pltpu.VMEM((2 * height, 128), f32),
            pltpu.VMEM((nb, 2, height, latent), bf16),
            pltpu.VMEM((nb, height, latent), bf16),
            pltpu.VMEM((nb, 2, 8, 128), f32),
            pltpu.VMEM((nb, 8, 128), f32),
            pltpu.VMEM((nb, height, latent), bf16),
            pltpu.VMEM((nb, height, latent), bf16),
            pltpu.VMEM((nb, 8, 128), f32),
            pltpu.VMEM((nb, 8, 128), f32),
            pltpu.VMEM((latent // 128, height, 128), f32),
            pltpu.VMEM((2, 2 * groups, half * VHEAD), bf16),
            pltpu.VMEM((groups, width), f32),
            pltpu.VMEM((hc, groups, width), f32),
            dma((4,)),
        ]
        + [dma((nb,)) for _ in range(14)]
        + [dma((1,)), dma((1,)), dma((hc,)), dma((hc,))],
        compiler_params=pltpu.CompilerParams(
            collective_id=0, has_side_effects=True, vmem_limit_bytes=56 * 1024 * 1024
        ),
    )(ids, bias, new_bias, q, kv, cache, w_uv, w_out)
    return out.reshape(rows // hc, 2, width)


def solution(mesh):
    return jax.shard_map(
        local,
        mesh=mesh,
        in_specs=(
            P(("groups", "branch"), None, "head", None),
            P(("groups", "branch"), None, None),
            P(("groups", "branch", "seq"), None, None),
            P("groups", None),
            P("groups"),
            P("groups"),
            P("head", None, None),
            P("head", "seq"),
        ),
        out_specs=P(("groups", "branch", "head"), None, "seq"),
        check_vma=False,
    )
```

time: 152 us -> 74.6 us (0.49)
  Pallas kernels: 0 us -> 50.9 us
  blocking collectives: 41.6 us -> 0 us
  matrix products: 32.8 us -> 0 us
  other arithmetic: 19.9 us -> 3.57 us
  between operations: 14.2 us -> 0.07 us
  starting transfers between devices: 9.73 us -> 0 us
  local copies, waits for them, and re-layouts: 28 us -> 19.4 us
  waiting for transfers between devices: 5.13 us -> 0 us
    pallas_call x0 -> x1, Pallas kernels: none -> 50.9 us  [local(): pl.pallas_call(functools.partial(kernel, scale, rows), out_shape=jax.Shap...]
    all_gather x2 -> x0, blocking collectives: 33.3 us -> none  [the longest x1 31.2 us: local(): new_keys = lax.all_gather(kv_new, 'branch', axis=0, tiled=True)]
    dot_general x6 -> x0, matrix products: 32.8 us -> none  [the longest x1 11.2 us: local(): jnp.einsum('brtha,bka->brthk', everyone, keys, preferred_element_type=jnp...]
    gather x2 -> x0, local copies, waits for them, and re-layouts: 23.9 us -> none  [local(): jnp.take(cache, ids.reshape(-1), axis=0)]
    unnamed x18 -> x3, local copies, waits for them, and re-layouts: 2.46 us -> 14.1 us
    all_to_all x2 -> x0, starting transfers between devices: 9.73 us -> none  [the longest x1 5.97 us: local(): summed = lax.all_to_all(summed, 'branch', 0, 0, tiled=True)]
    select_n x3 -> x4, other arithmetic: 10.7 us -> 1.3 us  [the longest x1 0.68 us: slots_of(): bias = jnp.where(jnp.arange(block_len) < room[:, :, None], 0.0, LOW)]
    unnamed x1 -> x0, blocking collectives: 8.35 us -> none
  transfers between devices with their start and end apart: 4 -> 0, of which waited for: 2 -> 0; matrix products, arithmetic and copies ran while one was open for 29% -> 0% of each run, Pallas kernels for 0% -> 0%
where the time goes in v2:
time: 74.6 us; the launch traced here: 73.9 us
  Pallas kernels  50.9 us (68%)
  local copies, waits for them, and re-layouts  19.4 us (26%)
  other arithmetic  3.57 us (5%)
    pallas_call x1, Pallas kernels, local(): pl.pallas_call(functools.partial(kernel, scale, rows), out_shape=jax.Shap...  50.9 us
    unnamed x3, local copies, waits for them, and re-layouts  14.1 us
    reshape x1, local copies, waits for them, and re-layouts, local(): q = queries.reshape(groups, 2, half, feature).transpose(1, 0, 2, 3)  1.74 us

profile of v2, /device:TPU:0, one launch (start us, length us, event | category | flops | bytes accessed | tf_op | source)
XLA Modules:
  0.0 73.9 jit_solution(320926446723705732)
XLA Ops:
  0.0 0.7 dynamic_slice.3
  0.8 0.1 broadcast_compare_fusion.1
  0.9 0.6 or_select_fusion
  1.5 0.7 broadcast_subtract_fusion
  2.2 0.7 reshape.212
  2.9 0.6 pad.4.kv_ref
  3.5 0.1 convert_reduce_fusion
  3.7 0.1 select_reduce_fusion.1.ids_ref
  3.8 0.0 copy-start
  3.9 0.4 select_reduce_fusion
  4.3 0.7 multiply_subtract_fusion
  5.0 0.1 lt.82
  5.2 0.7 compare_select_fusion.bias_ref
  5.9 1.7 %copy.11 = bf16[8,2,16,576]{3,2,0,1:T(8,128)(2,1)} copy(bf16[8,2,16,576]{3,2,1,0:T(8,128)(2,1)} %bitcast.9) | data formatting | bytes 589824 | tf_op jit(solution)/shard_map/reshape | solution.py:325
  7.6 14.1 %copy.12.cache_ref = bf16[64,128,576]{2,1,0:T(8,128)(2,1)} copy(bf16[64,128,576]{1,2,0:T(8,128)(2,1)} %param.10) | data formatting | bytes 18874368 | tf_op args[2]
  21.7 0.0 copy-done
  21.7 50.9 %shard_map.82 = bf16[4,1792]{1,0:T(4,128)(2,1)} custom-call(s32[4,16]{1,0:T(4,128)} %copy-done, f32[4,4,2048]{2,1,0:T(4,128)} %compare_select_fusion.bias_ref, f32[8,64]{1,0:T(8,128)} %bitcast.11, bf16[2,128,576]{2,1,0:T(8,128)(2,1)} %bitcast.8, bf16[16,576]{1,0:T(8,128)(2,1)} %pad.4.kv_ref, bf16[64,128,576]{2,1,0:T(8,128)(2,1)} %copy.12.cache_ref, ...), custom_call_target="tpu_custom_call" | custom-call | tf_op jit(solution)/shard_map/pallas_call | solution.py:349
  72.6 1.3 %reshape.213 = bf16[2,2,1792]{2,1,0:T(2,128)(2,1)} reshape(bf16[4,1792]{1,0:T(4,128)(2,1)} %shard_map.82) | data formatting | bytes 28672 | tf_op jit(solution)/shard_map/reshape | solution.py:393
  (10 shorter events, 0.1 us)
Async XLA Ops:
  3.8 17.8 %copy-start = (s32[4,16]{1,0:T(4,128)}, s32[4,16]{1,0:T(4,128)S(1)}, u32[]{:S(2)}) copy-start(s32[4,16]{1,0:T(4,128)S(1)} %select_reduce_fusion.1.ids_ref) | copy-start | bytes 772

commit v3 on v2

--- a/solution.py
+++ b/solution.py
@@ -13,24 +13,6 @@
 LOW = -1e30
 
 
-def slots_of(block_list, lengths, my_index, block_count, block_len, rows, slots):
-    mine = block_list - my_index * block_count
-    lead = mine[::rows]
-    held = (lead >= 0) & (lead < block_count)
-    spots = jnp.arange(mine.shape[1])
-    before = spots[None, :] < spots[:, None]
-    rank = jnp.sum((held[:, None, :] & before[None]).astype(jnp.int32), axis=2)
-    slot = jnp.arange(slots)
-    chosen = held[:, None, :] & (rank[:, None, :] == slot[None, :, None])
-    ids = jnp.sum(jnp.where(chosen, lead[:, None, :], 0), axis=2)
-    all_ids = jnp.repeat(ids, rows, axis=0)
-    match = mine[:, None, :] == all_ids[:, :, None]
-    place = jnp.sum(jnp.where(match, spots, 0), axis=2)
-    room = lengths[:, None] - place * block_len
-    bias = jnp.where(jnp.arange(block_len) < room[:, :, None], 0.0, LOW)
-    return ids, bias.reshape(-1, rows, slots * block_len)
-
-
 def as_row(column):
     short = 128 - column.shape[0]
     if short > 0:
@@ -54,9 +36,9 @@
 def kernel(
     scale,
     rows,
-    ids_ref,
-    bias_ref,
-    new_bias_ref,
+    list_ref,
+    lengths_ref,
+    parent_ref,
     q_ref,
     kv_ref,
     cache_ref,
@@ -81,6 +63,10 @@
     zs_out,
     zs_in,
     latent_v,
+    ids_v,
+    ids_s,
+    bias_v,
+    kv_v,
     head_v,
     red_out,
     red_in,
@@ -107,27 +93,23 @@
     nb, hc = lax.axis_size("branch"), lax.axis_size("head")
     z, x, core = lax.axis_index("branch"), lax.axis_index("head"), lax.axis_index("seq")
     other = 1 - core
-    height, feature = q_ref.shape[1], q_ref.shape[2]
-    block_len = cache_v.shape[1]
-    slots = ids_ref.shape[1]
+    block_count, feature, block_len = cache_v.shape
+    branches, list_len = list_ref.shape
+    slots = list_len // (nb * 2)
     latent = uv_v.shape[1]
     heads = uv_v.shape[0]
     groups = rows * 2
+    height = groups * heads
+
+    def q_half(g):
+        if len(q_ref.shape) == 4:
+            return q_ref.at[g]
+        return q_ref.at[:, pl.ds(pl.multiple_of(g * heads, heads), heads), :]
 
     cache_copy = pltpu.make_async_copy(cache_ref, cache_v, local_sem.at[0])
     cache_copy.start()
     uv_copy = pltpu.make_async_copy(uv_ref.at[pl.ds(core * heads, heads)], uv_v, local_sem.at[1])
     uv_copy.start()
-    depth = out_v.shape[1]
-    out_copies = []
-    for g in range(2):
-        out_copies.append(
-            pltpu.make_async_copy(
-                out_w_ref.at[pl.ds(g * depth, depth)], out_v.at[g], local_sem.at[2 + g]
-            )
-        )
-        out_copies[-1].start()
-
     barrier = pltpu.get_barrier_semaphore()
     for d in range(1, nb):
         pl.semaphore_signal(
@@ -138,6 +120,10 @@
             barrier, inc=1, device_id={"head": lax.rem(x + e, hc)}, device_id_type=MESH
         )
     pl.semaphore_signal(barrier, inc=1, device_id={"seq": other}, device_id_type=MESH)
+
+    drafts = [kv_ref[r].astype(jnp.float32) for r in range(rows)]
+    drafts.append(jnp.zeros((kv_v.shape[0] - groups, feature), jnp.float32))
+    kv_v[...] = jnp.concatenate(drafts, axis=0).astype(jnp.bfloat16)
     pl.semaphore_wait(barrier, nb - 1 + hc - 1 + 1)
 
     def remote(src, dst, send, recv, target):
@@ -161,28 +147,67 @@
     for d in range(1, nb):
         there = {"branch": lax.rem(z + d, nb)}
         q_copies.append(
-            go(remote(q_ref.at[core], q_all.at[d, core], q_send.at[d], q_recv.at[d], there))
+            go(remote(q_half(core), q_all.at[d, core], q_send.at[d], q_recv.at[d], there))
         )
     for d in range(1, nb):
         there = {"branch": lax.rem(z + d, nb)}
-        kv_copies.append(go(remote(kv_ref, kv_all.at[d], kv_send.at[d], kv_recv.at[d], there)))
-    kv_all[0] = kv_ref[...]
+        kv_copies.append(go(remote(kv_v, kv_all.at[d], kv_send.at[d], kv_recv.at[d], there)))
+    kv_all[0] = kv_v[...]
+
+    mine = list_ref[...] - (z * 2 + core) * block_count
+    lead = jnp.concatenate(
+        [
+            jnp.broadcast_to(mine[i * rows : i * rows + 1], (rows, list_len))
+            for i in range(nb)
+        ],
+        axis=0,
+    )
+    held = (lead >= 0) & (lead < block_count)
+    spots = lax.broadcasted_iota(jnp.int32, (branches, list_len), 1)
+    line = lax.broadcasted_iota(jnp.int32, (branches, list_len), 0)
+    counted = held.astype(jnp.int32)
+    rank = counted
+    step = 1
+    while step < list_len:
+        rank = rank + jnp.where(spots >= step, pltpu.roll(rank, step, 1), 0)
+        step *= 2
+    rank = jnp.where(held, rank - 1, -1)
+    reach = jnp.zeros((branches, list_len), jnp.int32)
+    for b in range(branches):
+        reach = jnp.where(line == b, lengths_ref[b], reach)
+    table = jnp.zeros((branches, list_len), jnp.int32)
+    picks = []
+    for s in range(slots):
+        pick = jnp.sum(jnp.where(rank == s, lead, 0), axis=1, keepdims=True)
+        picks.append(pick)
+        table = jnp.where(spots == s, pick, table)
+    ids_v[...] = table
+    ids_copy = pltpu.make_async_copy(ids_v, ids_s, local_sem.at[4])
+    ids_copy.start()
+    for s in range(slots):
+        place = jnp.sum(jnp.where(mine == picks[s], spots, 0), axis=1, keepdims=True)
+        seen = spots + place * block_len < reach
+        bias_v[:, s * block_len : (s + 1) * block_len] = jnp.where(seen, 0.0, LOW)
+    ids_copy.wait()
 
     o_copies, s_copies, z_copies, zs_copies = [], [], [None], [None]
 
     def attend(d):
         source = lax.rem(z + nb - d, nb)
         for s in range(slots):
-            keys[s * block_len : (s + 1) * block_len, :] = cache_v[ids_ref[source, s]]
-        q = (q_ref if d == 0 else q_all.at[d])[...].reshape(2 * height, feature)
-        scores[...] = lax.dot_general(
-            q, keys[...], (((1,), (1,)), ((), ())), preferred_element_type=jnp.float32
-        )
+            keys[:, s * block_len : (s + 1) * block_len] = cache_v[ids_s[source * rows, s]]
+        if d == 0:
+            q = jnp.concatenate(
+                [q_half(g)[...].reshape(height, feature) for g in range(2)], axis=0
+            )
+        else:
+            q = q_all[d].reshape(2 * height, feature)
+        scores[...] = jnp.dot(q, keys[...], preferred_element_type=jnp.float32)
         size = height // rows
         for g in range(2):
             for r in range(rows):
                 at = g * height + r * size
-                v = scores[at : at + size, :] * scale + bias_ref[source, r : r + 1, :]
+                v = scores[at : at + size, :] * scale + bias_v[pl.ds(source * rows + r, 1), :]
                 peak = jnp.max(v, axis=1, keepdims=True)
                 p = jnp.exp2(v - peak)
                 total = jnp.sum(p, axis=1, keepdims=True)
@@ -191,7 +216,12 @@
                 column[at : at + size, :] = jnp.where(lane == 0, peak, total)
         for g in range(2):
             s_out[d, g] = as_row(column[g * height : (g + 1) * height, :])
-        summed = jnp.dot(probs[...], keys[:, :latent], preferred_element_type=jnp.float32)
+        summed = lax.dot_general(
+            probs[...],
+            keys[:latent, :],
+            (((1,), (1,)), ((), ())),
+            preferred_element_type=jnp.float32,
+        )
         o_out[d] = summed.astype(jnp.bfloat16).reshape(2, height, latent)
         partner = {"seq": other}
         s_copies.append(go(remote(s_out.at[d, other], s_in.at[d], s_send.at[d], s_recv.at[d], partner)))
@@ -219,6 +249,15 @@
             z_copies.append(go(remote(z_out.at[d], z_in.at[d], z_send.at[d], z_recv.at[d], there)))
 
     cache_copy.wait()
+    depth = out_v.shape[1]
+    out_copies = []
+    for g in range(2):
+        out_copies.append(
+            pltpu.make_async_copy(
+                out_w_ref.at[pl.ds(g * depth, depth)], out_v.at[g], local_sem.at[2 + g]
+            )
+        )
+        out_copies[-1].start()
     forwards = [None]
     attend(0)
     for d in range(1, nb):
@@ -238,9 +277,22 @@
     new_keys = kv_all[...].reshape(-1, feature)
     size = height // groups
     new_scores = lax.dot_general(
-        q_ref[core], new_keys, (((1,), (1,)), ((), ())), preferred_element_type=jnp.float32
+        q_half(core)[...].reshape(height, feature), new_keys, (((1,), (1,)), ((), ())), preferred_element_type=jnp.float32
     )
-    new_v = new_scores.reshape(groups, size, -1) * scale + new_bias_ref[...][:, None, :]
+    pad = kv_v.shape[0]
+    extent = (groups, nb * pad)
+    spot = lax.broadcasted_iota(jnp.int32, extent, 1)
+    entry = lax.broadcasted_iota(jnp.int32, extent, 0)
+    origin = z - spot // pad
+    origin = jnp.where(origin < 0, origin + nb, origin)
+    inner = spot % pad
+    which = jnp.where(inner < groups, origin * rows + inner // 2, -2)
+    above = jnp.full(extent, -1, jnp.int32)
+    for r in range(rows):
+        above = jnp.where(entry // 2 == r, parent_ref[z * rows + r], above)
+    seen = (which == above) | ((which == z * rows + entry // 2) & (inner % 2 <= entry % 2))
+    new_bias = jnp.where(seen, 0.0, LOW)
+    new_v = new_scores.reshape(groups, size, -1) * scale + new_bias[:, None, :]
     new_v = new_v.reshape(height, -1)
     new_peak = jnp.max(new_v, axis=1, keepdims=True)
     new_p = jnp.exp2(new_v - new_peak)
@@ -298,11 +350,12 @@
     for e in range(1, hc):
         reds[e - 1].wait_recv()
         result = result + red_in[e - 1]
-    count = out_ref.shape[0]
-    mine = jnp.zeros(out_ref.shape, jnp.float32)
+    count = groups // hc
+    kept = jnp.zeros((count, result.shape[1]), jnp.float32)
     for k in range(hc):
-        mine = jnp.where(x == k, result[k * count : (k + 1) * count], mine)
-    out_ref[...] = mine.astype(out_ref.dtype)
+        kept = jnp.where(x == k, result[k * count : (k + 1) * count], kept)
+    for k in range(count // 2):
+        out_ref[k] = kept[2 * k : 2 * k + 2].astype(out_ref.dtype)
     for copy in sent:
         copy.wait_send()
 
@@ -314,45 +367,30 @@
     nb = lax.axis_size("branch")
     ns = lax.axis_size("seq")
     hc = lax.axis_size("head")
-    branch_at = lax.axis_index("branch")
-    my_index = branch_at * ns + lax.axis_index("seq")
     slots = block_list.shape[1] // (nb * ns)
     scale = float(VHEAD + ROPE) ** (-0.5) * 1.4426950408889634
-    ids, bias = slots_of(block_list, lengths, my_index, block_count, block_len, rows, slots)
     half = heads // 2
     groups = rows * 2
     height = groups * half
-    q = queries.reshape(groups, 2, half, feature).transpose(1, 0, 2, 3)
-    q = q.reshape(2, height, feature)
+    q = queries.reshape(groups, heads, feature)
+    if half % 16 != 0:
+        q = q.reshape(groups, 2, half, feature).transpose(1, 0, 2, 3)
     pad = 16
-    kv = jnp.pad(kv_new.reshape(groups, feature), ((0, pad - groups), (0, 0)))
-
-    parents = lax.dynamic_slice_in_dim(parent, branch_at * rows, rows)
-    spot = jnp.arange(nb * pad)
-    origin = (branch_at - spot // pad + nb) % nb
-    inner = spot % pad
-    which = jnp.where(inner < groups, origin * rows + inner // 2, -2)
-    own = branch_at * rows + jnp.arange(rows)
-    seen = (which[None, None, :] == parents[:, None, None]) | (
-        (which[None, None, :] == own[:, None, None])
-        & ((inner % 2)[None, None, :] <= jnp.arange(2)[None, :, None])
-    )
-    new_bias = jnp.where(seen, 0.0, LOW).reshape(groups, nb * pad)
-
+    branches = block_list.shape[0]
     depth = w_out.shape[0] // 2
     width = w_out.shape[1]
     dma = pltpu.SemaphoreType.DMA
     vmem = pl.BlockSpec(memory_space=pltpu.VMEM)
     hbm = pl.BlockSpec(memory_space=pl.ANY)
-    count = groups // hc
+    smem = pl.BlockSpec(memory_space=pltpu.SMEM)
     bf16, f32 = jnp.bfloat16, jnp.float32
-    out = pl.pallas_call(
+    return pl.pallas_call(
         functools.partial(kernel, scale, rows),
-        out_shape=jax.ShapeDtypeStruct((count, width), bf16),
+        out_shape=jax.ShapeDtypeStruct((rows // hc, 2, width), bf16),
         in_specs=[
-            pl.BlockSpec(memory_space=pltpu.SMEM),
             vmem,
-            vmem,
+            smem,
+            smem,
             vmem,
             vmem,
             hbm,
@@ -361,12 +399,12 @@
         ],
         out_specs=vmem,
         scratch_shapes=[
-            pltpu.VMEM((block_count, block_len, feature), bf16),
+            pltpu.VMEM((block_count, feature, block_len), bf16),
             pltpu.VMEM((half, latent, VHEAD), bf16),
             pltpu.VMEM((2, depth, width), bf16),
-            pltpu.VMEM((nb, 2, height, feature), bf16),
+            pltpu.VMEM((nb, 2, groups, half, feature), bf16),
             pltpu.VMEM((nb, pad, feature), bf16),
-            pltpu.VMEM((slots * block_len, feature), bf16),
+            pltpu.VMEM((feature, slots * block_len), bf16),
             pltpu.VMEM((2 * height, slots * block_len), f32),
             pltpu.VMEM((2 * height, slots * block_len), bf16),
             pltpu.VMEM((2 * height, 128), f32),
@@ -379,18 +417,21 @@
             pltpu.VMEM((nb, 8, 128), f32),
             pltpu.VMEM((nb, 8, 128), f32),
             pltpu.VMEM((latent // 128, height, 128), f32),
+            pltpu.VMEM(block_list.shape, jnp.int32),
+            pltpu.SMEM(block_list.shape, jnp.int32),
+            pltpu.VMEM((branches, slots * block_len), f32),
+            pltpu.VMEM((pad, feature), bf16),
             pltpu.VMEM((2, 2 * groups, half * VHEAD), bf16),
             pltpu.VMEM((groups, width), f32),
             pltpu.VMEM((hc, groups, width), f32),
-            dma((4,)),
+            dma((5,)),
         ]
         + [dma((nb,)) for _ in range(14)]
         + [dma((1,)), dma((1,)), dma((hc,)), dma((hc,))],
         compiler_params=pltpu.CompilerParams(
             collective_id=0, has_side_effects=True, vmem_limit_bytes=56 * 1024 * 1024
         ),
-    )(ids, bias, new_bias, q, kv, cache, w_uv, w_out)
-    return out.reshape(rows // hc, 2, width)
+    )(block_list, lengths, parent, q, kv_new, cache.swapaxes(1, 2), w_uv, w_out)
 
 
 def solution(mesh):

time: 74.6 us -> 52.5 us (0.70)
  local copies, waits for them, and re-layouts: 19.4 us -> 1.32 us
  other arithmetic: 3.57 us -> 0 us
    unnamed x3 -> x1, local copies, waits for them, and re-layouts: 14.1 us -> 1.32 us
    reshape x3 -> x0, local copies, waits for them, and re-layouts: 3.78 us -> none  [the longest x1 1.74 us: local(): q = queries.reshape(groups, 2, half, feature).transpose(1, 0, 2, 3)]
    sub x2 -> x0, other arithmetic: 1.43 us -> none  [the longest x1 0.73 us: slots_of(): room = lengths[:, None] - place * block_len]
    select_n x4 -> x0, other arithmetic: 1.3 us -> none  [the longest x1 0.68 us: slots_of(): bias = jnp.where(jnp.arange(block_len) < room[:, :, None], 0.0, LOW)]
where the time goes in v3:
time: 52.5 us; the launch traced here: 52.2 us
  Pallas kernels  50.9 us (97%)
  local copies, waits for them, and re-layouts  1.32 us (3%)
    pallas_call x1, Pallas kernels, local(): pl.pallas_call(functools.partial(kernel, scale, rows), out_shape=jax.Shap...  50.9 us
    unnamed x1, local copies, waits for them, and re-layouts  1.32 us

profile of v3, /device:TPU:0, one launch (start us, length us, event | category | flops | bytes accessed | tf_op | source)
XLA Modules:
  0.0 52.2 jit_solution(16082721429874339360)
XLA Ops:
  0.0 50.9 %shard_map.82 = bf16[2,2,1792]{2,1,0:T(2,128)(2,1)} custom-call(s32[16,128]{1,0:T(8,128)} %list_ref.1, s32[16]{0:T(128)} %lengths_ref.1, s32[16]{0:T(128)} %parent_ref.1, bf16[8,32,576]{2,1,0:T(8,128)(2,1)} %bitcast.3, bf16[4,2,576]{2,1,0:T(2,128)(2,1)} %kv_ref.1, bf16[64,576,128]{2,1,0:T(8,128)(2,1)} %bitcast.2, bf16[32,512,128]{2,1,0:T(8,128)(2,1)} %uv_ref.1, ...), custom_call_target="tpu_custom_call" | custom-call | tf_op jit(solution)/shard_map/pallas_call | solution.py:387
  50.9 1.3 %copy.10 = bf16[2,2,1792]{2,1,0:T(2,128)(2,1)} copy(bf16[2,2,1792]{2,1,0:T(2,128)(2,1)} %shard_map.82) | data formatting | bytes 28672

commit v4 on v3

--- a/solution.py
+++ b/solution.py
@@ -143,12 +143,36 @@
         sent.append(copy)
         return copy
 
-    q_copies, kv_copies = [None], [None]
-    for d in range(1, nb):
-        there = {"branch": lax.rem(z + d, nb)}
-        q_copies.append(
-            go(remote(q_half(core), q_all.at[d, core], q_send.at[d], q_recv.at[d], there))
-        )
+    kv_copies = [None]
+
+    def pass_on(d, act):
+        block = q_half(core) if d is None else q_all.at[d, core]
+        for way in (1, -1):
+            if d is None:
+                going = (z + 1 < nb) if way == 1 else (z > 0)
+                slot = 1 if way == 1 else nb - 1
+                sem = q_send.at[0] if way == 1 else q_send.at[nb]
+            else:
+                going = ((z >= d) & (z + 1 < nb)) if way == 1 else ((z < d) & (z > 0))
+                slot = jnp.clip(d + way, 1, nb - 1)
+                sem = q_send.at[d]
+            there = {"branch": jnp.clip(z + way, 0, nb - 1)}
+
+            @pl.when(going)
+            def _():
+                act(remote(block, q_all.at[slot, core], sem, q_recv.at[slot], there))
+
+    fewer = jnp.minimum(z, nb - 1 - z)
+    left_more = z > nb - 1 - z
+
+    def nth(j):
+        pair = (j + 1) // 2
+        paired = pair if j % 2 == 1 else nb - pair
+        tail = jnp.where(left_more, j - fewer, nb - (j - fewer))
+        return jnp.where(j <= 2 * fewer, paired, tail)
+
+    order = [0] + [nth(j) for j in range(1, nb)]
+    pass_on(None, lambda copy: copy.start())
     for d in range(1, nb):
         there = {"branch": lax.rem(z + d, nb)}
         kv_copies.append(go(remote(kv_v, kv_all.at[d], kv_send.at[d], kv_recv.at[d], there)))
@@ -192,11 +216,12 @@
 
     o_copies, s_copies, z_copies, zs_copies = [], [], [None], [None]
 
-    def attend(d):
+    def attend(j):
+        d = order[j]
         source = lax.rem(z + nb - d, nb)
         for s in range(slots):
             keys[:, s * block_len : (s + 1) * block_len] = cache_v[ids_s[source * rows, s]]
-        if d == 0:
+        if j == 0:
             q = jnp.concatenate(
                 [q_half(g)[...].reshape(height, feature) for g in range(2)], axis=0
             )
@@ -227,8 +252,9 @@
         s_copies.append(go(remote(s_out.at[d, other], s_in.at[d], s_send.at[d], s_recv.at[d], partner)))
         o_copies.append(go(remote(o_out.at[d, other], o_in.at[d], o_send.at[d], o_recv.at[d], partner)))
 
-    def merge(d):
-        s_copies[d].wait_recv()
+    def merge(j):
+        d = order[j]
+        s_copies[j].wait_recv()
         one, two = s_out[d, core], s_in[d]
         top = jnp.maximum(one[0:1], two[0:1])
         c1, c2 = jnp.exp2(one[0:1] - top), jnp.exp2(two[0:1] - top)
@@ -236,12 +262,12 @@
         line = lax.broadcasted_iota(jnp.int32, zs_out.shape[1:], 0)
         zs_out[d] = jnp.where(line == 0, top, total)
         cols = as_columns([c1, c2], height)
-        o_copies[d].wait_recv()
+        o_copies[j].wait_recv()
         merged = o_out[d, core].astype(jnp.float32) * cols[:, 0:1] + o_in[d].astype(
             jnp.float32
         ) * cols[:, 1:2]
         z_out[d] = merged.astype(jnp.bfloat16)
-        if d > 0:
+        if j > 0:
             there = {"branch": lax.rem(z + nb - d, nb)}
             zs_copies.append(
                 go(remote(zs_out.at[d], zs_in.at[d], zs_send.at[d], zs_recv.at[d], there))
@@ -259,17 +285,22 @@
         )
         out_copies[-1].start()
     forwards = [None]
+
+    def receive(j):
+        d = order[j]
+        landed = q_all.at[d, core]
+        remote(landed, landed, q_send.at[d], q_recv.at[d], {"seq": other}).wait_recv()
+        pass_on(d, lambda copy: copy.start())
+        forwards.append(go(remote(landed, landed, f_send.at[d], f_recv.at[d], {"seq": other})))
+
     attend(0)
-    for d in range(1, nb):
-        q_copies[d].wait_recv()
-        forward = go(
-            remote(
-                q_all.at[d, core], q_all.at[d, core], f_send.at[d], f_recv.at[d], {"seq": other}
-            )
-        )
-        merge(d - 1)
-        forward.wait_recv()
-        attend(d)
+    receive(1)
+    for j in range(1, nb):
+        if j + 1 < nb:
+            receive(j + 1)
+        merge(j - 1)
+        forwards[j].wait_recv()
+        attend(j)
     merge(nb - 1)
 
     for d in range(1, nb):
@@ -304,7 +335,7 @@
 
     stats = [zs_out[0], new_row]
     for d in range(1, nb):
-        zs_copies[d].wait_recv()
+        remote(zs_out.at[d], zs_in.at[d], zs_send.at[d], zs_recv.at[d], {"seq": other}).wait_recv()
         stats.append(zs_in[d])
     top = functools.reduce(jnp.maximum, [s[0:1] for s in stats])
     shares = [jnp.exp2(s[0:1] - top) for s in stats]
@@ -312,7 +343,7 @@
     cols = as_columns([c / total for c in shares], height)
     latent_out = z_out[0].astype(jnp.float32) * cols[:, 0:1] + new_sum * cols[:, 1:2]
     for d in range(1, nb):
-        z_copies[d].wait_recv()
+        remote(z_out.at[d], z_in.at[d], z_send.at[d], z_recv.at[d], {"seq": other}).wait_recv()
         latent_out = latent_out + z_in[d].astype(jnp.float32) * cols[:, d + 1 : d + 2]
     for j in range(latent // 128):
         latent_v[j] = latent_out[:, j * 128 : (j + 1) * 128]
@@ -358,6 +389,9 @@
         out_ref[k] = kept[2 * k : 2 * k + 2].astype(out_ref.dtype)
     for copy in sent:
         copy.wait_send()
+    pass_on(None, lambda copy: copy.wait_send())
+    for j in range(1, nb):
+        pass_on(order[j], lambda copy: copy.wait_send())
 
 
 def local(queries, kv_new, cache, block_list, lengths, parent, w_uv, w_out):
@@ -426,7 +460,7 @@
             pltpu.VMEM((hc, groups, width), f32),
             dma((5,)),
         ]
-        + [dma((nb,)) for _ in range(14)]
+        + [dma((nb + 1,)) for _ in range(14)]
         + [dma((1,)), dma((1,)), dma((hc,)), dma((hc,))],
         compiler_params=pltpu.CompilerParams(
             collective_id=0, has_side_effects=True, vmem_limit_bytes=56 * 1024 * 1024

time: 52.5 us -> 43.4 us (0.83)
  Pallas kernels: 50.9 us -> 41.9 us
    pallas_call x1, Pallas kernels: 50.9 us -> 41.9 us  [local(): pl.pallas_call(functools.partial(kernel, scale, rows), out_shape=jax.Shap...]
where the time goes in v4:
time: 43.4 us; the launch traced here: 43.2 us
  Pallas kernels  41.9 us (97%)
  local copies, waits for them, and re-layouts  1.32 us (3%)
    pallas_call x1, Pallas kernels, local(): pl.pallas_call(functools.partial(kernel, scale, rows), out_shape=jax.Shap...  41.9 us
    unnamed x1, local copies, waits for them, and re-layouts  1.32 us

profile of v4, /device:TPU:0, one launch (start us, length us, event | category | flops | bytes accessed | tf_op | source)
XLA Modules:
  0.0 43.2 jit_solution(18308385915031341277)
XLA Ops:
  0.0 41.9 %shard_map.82 = bf16[2,2,1792]{2,1,0:T(2,128)(2,1)} custom-call(s32[16,128]{1,0:T(8,128)} %list_ref.1, s32[16]{0:T(128)} %lengths_ref.1, s32[16]{0:T(128)} %parent_ref.1, bf16[8,32,576]{2,1,0:T(8,128)(2,1)} %bitcast.3, bf16[4,2,576]{2,1,0:T(2,128)(2,1)} %kv_ref.1, bf16[64,576,128]{2,1,0:T(8,128)(2,1)} %bitcast.2, bf16[32,512,128]{2,1,0:T(8,128)(2,1)} %uv_ref.1, ...), custom_call_target="tpu_custom_call" | custom-call | tf_op jit(solution)/shard_map/pallas_call | solution.py:421
  41.9 1.3 %copy.10 = bf16[2,2,1792]{2,1,0:T(2,128)(2,1)} copy(bf16[2,2,1792]{2,1,0:T(2,128)(2,1)} %shard_map.82) | data formatting | bytes 28672
